TPU v7x, 256 devices: a whole 4x4x8 slice. The times are simulated.
256 devices in a mesh: pipe: 4 (over x), seq: 32 (over z, y), batch: 2 (over core).
Axes of the slice: x: 4, y: 4, z: 8, core: 2. Of those that a mesh axis runs over, the one named last changes fastest.
Arguments:
- latent_noise: float32 [4, 2, 512, 64], P('pipe', 'batch', 'seq'), may hold values from -6 to 6
- text_rows: bfloat16 [4, 2, 256, 4096], P(None, 'batch', None, 'seq'), may hold values from -6 to 6
- text_lengths: int32 [4, 2], P(None, 'batch'), may hold values from 32 to 256, as said below
- plan: int32 [3], replicated, may hold values from 1 to 1000, as said below
- context_weight: bfloat16 [4096, 1536], P('seq'), may hold values from -0.09375 to 0.09375
- w_embed: bfloat16 [64, 1536], replicated, may hold values from -0.75 to 0.75
- w_attention: bfloat16 [4, 1536, 4608], P('pipe', 'batch'), may hold values from -1 to 1
- w_project: bfloat16 [4, 1536, 1536], P('pipe', 'batch'), may hold values from -0.15625 to 0.15625
- w_modulate: bfloat16 [4, 256, 4608], P('pipe', 'batch'), may hold values from -0.375 to 0.375
- w_final: bfloat16 [1536, 64], replicated, may hold values from -0.15625 to 0.15625
Outputs:
- final_latent: float32 [4, 2, 512, 64], P('pipe', 'batch', 'seq')
Inputs may be any that keep to these rules, and one draw needn't show every extreme that they name: `text_lengths`: at least one prompt has 256 live rows and one has 32. `plan`: strictly falling; the first entry is 1000 and the last is 1.
All inputs are finite; a program needn't handle non-finite values.
Results may differ from a plain program's by a relative error of at most 0.02.
Values may be sent and summed in bfloat16 or wider, within the bound.
No kernel may reach another device: no remote copies, remote signals or barrier semaphores. Data moves between devices by JAX's collectives and lax.ppermute only.
A program may use at most 128 MiB of HBM per device.

v0:
```python
import math
import jax
import jax.numpy as jnp
from jax import lax
from jax.sharding import PartitionSpec as P

HEADS = 16
STEPS = 2
epsilon = 1e-06


def shifted(value, axis, by):
    peers = lax.axis_size(axis)
    return lax.ppermute(value, axis, [(i, (i + by) % peers) for i in range(peers)])


def layer_norm(hidden):
    values = hidden.astype(jnp.float32)
    center = values - jnp.mean(values, axis=-1, keepdims=True)
    spread = jnp.mean(center * center, axis=-1, keepdims=True)
    return center * lax.rsqrt(spread + epsilon)


def time_features(noise_level, feature_count):
    half_count = feature_count // 2
    wave_frequency = jnp.exp(
        -math.log(10000.0) * jnp.arange(half_count, dtype=jnp.float32) / half_count
    )
    angles = noise_level * wave_frequency
    return jnp.concatenate([jnp.cos(angles), jnp.sin(angles)]).astype(jnp.bfloat16)


def on_device(
    latent_noise,
    text_rows,
    text_lengths,
    plan,
    context_weight,
    w_embed,
    w_attention,
    w_project,
    w_modulate,
    w_final,
):
    seq_count = lax.axis_size("seq")
    device_count = lax.axis_size("pipe")
    section = lax.axis_index("pipe")
    tokens_here = latent_noise.shape[2]
    text_total = text_rows.shape[2]
    text_here = text_total // seq_count
    model_width = w_embed.shape[1]
    gathered = (
        lax.all_gather(w_attention, "batch", axis=1, tiled=True),
        lax.all_gather(w_project, "batch", axis=1, tiled=True),
        lax.all_gather(w_modulate, "batch", axis=1, tiled=True),
    )
    attn_weight = gathered[0][0]
    proj_weight = gathered[1][0]
    mod_weight = gathered[2][0]
    inner_width = proj_weight.shape[0]
    head_size = inner_width // HEADS
    unit_count = max(HEADS, seq_count)
    replica_count = unit_count // HEADS
    unit_here = unit_count // seq_count
    query_rows = tokens_here // replica_count
    factor = 1.0 / math.sqrt(head_size)
    resident_text = text_rows[:, 0]
    context = lax.psum_scatter(
        jnp.einsum(
            "ipe,ea->pia", resident_text, context_weight, preferred_element_type=jnp.float32
        ),
        "seq",
        scatter_dimension=0,
        tiled=True,
    ).astype(jnp.bfloat16)
    live_text = jnp.arange(text_total)[None, :] < text_lengths[:, 0][:, None]

    def key_units(key_rows):
        row_count = key_rows.shape[0]
        heads_first = key_rows.reshape(row_count, HEADS, head_size).transpose(1, 0, 2)
        return jnp.repeat(heads_first, replica_count, axis=0).reshape(
            unit_count, row_count * head_size
        )

    def query_units(query_block):
        parted = query_block.reshape(replica_count, query_rows, HEADS, head_size).transpose(
            2, 0, 1, 3
        )
        return parted.reshape(unit_count, query_rows * head_size)

    def from_units(blocks):
        parted = blocks.reshape(HEADS, replica_count, query_rows, head_size).transpose(1, 2, 0, 3)
        return parted.reshape(tokens_here, inner_width)

    def split_joined(moved):
        parted = moved.reshape(unit_here, seq_count, tokens_here + text_here, head_size)
        image_part = parted[:, :, :tokens_here].reshape(
            unit_here, seq_count * tokens_here, head_size
        )
        text_part = parted[:, :, tokens_here:].reshape(unit_here, seq_count * text_here, head_size)
        return jnp.concatenate([image_part, text_part], 1)

    text_scale_weight = attn_weight[:, inner_width:]

    def one_turn(turn_index, state_pair):
        hidden, latent = state_pair
        anchor = (section - turn_index) % device_count
        entry_turn = (device_count - anchor) % device_count
        passed = turn_index - entry_turn
        active = (passed >= 0) & (passed < STEPS * device_count)
        step_index = jnp.clip(passed // device_count, 0, STEPS - 1)
        positions = jnp.arange(STEPS + 1)
        noise_level = jnp.sum(jnp.where(positions == step_index, plan, 0)).astype(jnp.float32)
        next_level = jnp.sum(jnp.where(positions == step_index + 1, plan, 0)).astype(jnp.float32)
        features = time_features(noise_level, mod_weight.shape[0])
        modulation = jnp.dot(features[None, :], mod_weight, preferred_element_type=jnp.float32)[0]
        mod_shift = modulation[:model_width]
        mod_scale = modulation[model_width : 2 * model_width]
        mod_gate = modulation[2 * model_width :]
        embedded = jnp.dot(
            latent.astype(jnp.bfloat16), w_embed, preferred_element_type=jnp.float32
        ).astype(jnp.bfloat16)
        incoming = jnp.where(section == 0, embedded, hidden)
        normed = (layer_norm(incoming) * (1.0 + mod_scale) + mod_shift).astype(jnp.bfloat16)
        projected = jnp.dot(normed, attn_weight, preferred_element_type=jnp.float32).astype(
            jnp.bfloat16
        )
        queries = query_units(projected[:, :inner_width])
        image_keys = projected[:, inner_width : 2 * inner_width]
        image_values = projected[:, 2 * inner_width :]
        live_keys = lax.dynamic_index_in_dim(live_text, anchor, 0, keepdims=False)
        context_rows = lax.dynamic_index_in_dim(context, anchor, 1, keepdims=False)
        text_pairs = jnp.dot(
            context_rows, text_scale_weight, preferred_element_type=jnp.float32
        ).astype(jnp.bfloat16)
        joined_keys = jnp.concatenate([image_keys, text_pairs[:, :inner_width]], 0)
        joined_values = jnp.concatenate([image_values, text_pairs[:, inner_width:]], 0)
        got_queries, got_keys, got_values = (
            lax.all_to_all(queries, "seq", split_axis=0, concat_axis=1, tiled=True),
            lax.all_to_all(key_units(joined_keys), "seq", split_axis=0, concat_axis=1, tiled=True),
            lax.all_to_all(
                key_units(joined_values), "seq", split_axis=0, concat_axis=1, tiled=True
            ),
        )
        all_keys = split_joined(got_keys)
        all_values = split_joined(got_values)
        query_heads = got_queries.reshape(unit_here, seq_count * query_rows, head_size)
        scores = (
            jnp.einsum("uqc,ukc->uqk", query_heads, all_keys, preferred_element_type=jnp.float32)
            * factor
        )
        key_mask = jnp.concatenate([jnp.ones((seq_count * tokens_here,), dtype=bool), live_keys])
        scores = jnp.where(key_mask[None, None, :], scores, -1e30)
        highest = jnp.max(scores, axis=-1, keepdims=True)
        exponents = jnp.exp(scores - highest)
        totals = jnp.sum(exponents, axis=-1, keepdims=True)
        weights = (exponents / totals).astype(jnp.bfloat16)
        attended = jnp.einsum(
            "uqk,ukc->uqc", weights, all_values, preferred_element_type=jnp.float32
        ).astype(jnp.bfloat16)
        returned = lax.all_to_all(
            attended.reshape(unit_here, seq_count * query_rows * head_size),
            "seq",
            split_axis=1,
            concat_axis=0,
            tiled=True,
        )
        merged_heads = from_units(returned)
        update = jnp.dot(merged_heads, proj_weight, preferred_element_type=jnp.float32)
        updated = (incoming.astype(jnp.float32) + mod_gate * update).astype(jnp.bfloat16)
        normed_out = layer_norm(updated).astype(jnp.bfloat16)
        velocity = jnp.dot(normed_out, w_final, preferred_element_type=jnp.float32)
        stepped = latent + (next_level - noise_level) / 1000.0 * velocity
        new_latent = jnp.where(active & (section == device_count - 1), stepped, latent)
        new_hidden = jnp.where(active, updated, hidden)
        sent_hidden, sent_latent = (
            shifted(new_hidden.astype(jnp.float32).astype(jnp.bfloat16), "pipe", 1).astype(
                jnp.float32
            ),
            shifted(new_latent.astype(jnp.bfloat16), "pipe", 1).astype(new_latent.dtype),
        )
        return (sent_hidden.astype(jnp.bfloat16), sent_latent)

    start_hidden = jnp.zeros((tokens_here, model_width), jnp.bfloat16)
    final_pair = lax.fori_loop(
        0, device_count * (STEPS + 1), one_turn, (start_hidden, latent_noise[0, 0])
    )
    return final_pair[1].reshape(latent_noise.shape)


def solution(mesh):
    placed = (
        P("pipe", "batch", "seq", None),
        P(None, "batch", None, "seq"),
        P(None, "batch"),
        P(),
        P("seq", None),
        P(),
        P("pipe", "batch", None),
        P("pipe", "batch", None),
        P("pipe", "batch", None),
        P(),
    )
    return jax.shard_map(
        on_device,
        mesh=mesh,
        in_specs=placed,
        out_specs=P("pipe", "batch", "seq", None),
        check_vma=False,
    )
```

profile of v0, /device:TPU:8, one launch (start us, length us, event | category | flops | bytes accessed | tf_op | source)
XLA Modules:
  0.0 1279.3 jit_solution(2273198371216502025)
XLA Ops:
  21.8 181.0 %all-reduce.3 = bf16[256,4,1536]{2,1,0:T(4,128)(2,1)S(1)} all-reduce(f32[256,4,1536]{2,1,0:T(4,128)} %copy.42), channel_id=2, replica_groups=mesh['pipe'=4,'seq'=32,'batch'=2] {'seq'}, use_global_device_ids=true, to_apply=%region_0.0.clone | all-reduce | flops 1572864 | bytes 9437184
  203.0 8.1 slice.137
  211.2 1061.0 %while.17 = (s32[]{:T(128)}, bf16[16,1536]{1,0:T(8,128)(2,1)S(1)}, f32[16,64]{1,0:T(8,128)S(1)}, s32[]{:T(128)}, pred[]{:T(512)}, /*index=5*/bf16[64,1536]{1,0:T...) while((s32[]{:T(128)}, bf16[16,1536]{1,0:T(8,128)(2,1)S(1)}, ...), condition=%wide.region_10.11_spmd, body=%wide.region_1.10_spmd.sunk | while | flops 464863840 | bytes 43831728 | solution.py:185
  224.6 9.6 all-to-all-start
  242.9 9.4 all-to-all-start.1
  286.4 8.1 all-to-all-done.3
  330.6 9.4 all-to-all-start.1
  374.1 8.1 all-to-all-done.3
  418.7 9.4 all-to-all-start.1
  462.2 8.1 all-to-all-done.3
  506.4 9.4 all-to-all-start.1
  549.9 8.1 all-to-all-done.3
  594.6 9.4 all-to-all-start.1
  638.2 8.1 all-to-all-done.3
  682.4 9.4 all-to-all-start.1
  725.9 8.1 all-to-all-done.3
  770.7 9.4 all-to-all-start.1
  858.4 9.4 all-to-all-start.1
  902.0 8.1 all-to-all-done.3
  946.7 9.4 all-to-all-start.1
  1035.0 9.4 all-to-all-start.1
  1123.2 9.4 all-to-all-start.1
  1210.9 9.4 all-to-all-start.1
  1254.5 8.1 all-to-all-done.3
  (1009 shorter events, 870.3 us)
Async XLA Ops:
  6.5 196.4 %all-gather.6.cloned.1.call-start = ((), (), s32[]{:S(2)}) async-start(), calls=%async_computation.5 | async-start | bytes 21233664 | tf_op jit(solution)/shard_map/all_gather | solution.py:53
  7.3 203.9 %all-gather.4.cloned.1.call-start = ((), (), s32[]{:S(2)}) async-start(), calls=%async_computation.4 | async-start | bytes 3538944 | tf_op jit(solution)/shard_map/all_gather | solution.py:55
  8.0 203.1 %all-gather.8.cloned.1.call-start = ((), (), s32[]{:S(2)}) async-start(), calls=%async_computation.6 | async-start | bytes 7077888 | tf_op jit(solution)/shard_map/all_gather | solution.py:54
  224.6 18.3 %all-to-all-start = ((bf16[32,2,384]{2,1,0:T(2,128)(2,1)}), bf16[32,2,384]{2,1,0:T(2,128)(2,1)S(1)}, u32[]{:S(2)}, u32[]{:S(2)}) async-start(bf16[32,2,384]{2,1,0:T(2,128)(2,1)} %reshape.315), calls=%async_computation | async-start | bytes 98304 | tf_op jit(solution)/shard_map/while/body/eval_jaxpr/all_to_all | solution.py:139
  242.9 18.3 %all-to-all-start.1 = ((bf16[32,2,1152]{2,1,0:T(2,128)(2,1)}), bf16[32,2,1152]{2,1,0:T(2,128)(2,1)S(1)}, u32[]{:S(2)}, u32[]{:S(2)}) async-start(bf16[32,2,1152]{2,1,0:T(2,128)(2,1)} %reshape.319), calls=%async_computation.1 | async-start | bytes 294912 | tf_op jit(solution)/shard_map/while/body/eval_jaxpr/all_to_all | solution.py:140
  261.2 14.5 %all-to-all-start.2 = ((bf16[32,2,1152]{2,1,0:T(2,128)(2,1)}), bf16[32,2,1152]{2,1,0:T(2,128)(2,1)S(1)}, u32[]{:S(2)}, u32[]{:S(2)}) async-start(bf16[32,2,1152]{2,1,0:T(2,128)(2,1)} %reshape.323), calls=%async_computation.2 | async-start | bytes 294912 | tf_op jit(solution)/shard_map/while/body/eval_jaxpr/all_to_all | solution.py:141
  330.6 18.3 %all-to-all-start.1 = ((bf16[32,2,1152]{2,1,0:T(2,128)(2,1)}), bf16[32,2,1152]{2,1,0:T(2,128)(2,1)S(1)}, u32[]{:S(2)}, u32[]{:S(2)}) async-start(bf16[32,2,1152]{2,1,0:T(2,128)(2,1)} %reshape.319), calls=%async_computation.1 | async-start | bytes 294912 | tf_op jit(solution)/shard_map/while/body/eval_jaxpr/all_to_all | solution.py:140
  418.7 18.3 %all-to-all-start.1 = ((bf16[32,2,1152]{2,1,0:T(2,128)(2,1)}), bf16[32,2,1152]{2,1,0:T(2,128)(2,1)S(1)}, u32[]{:S(2)}, u32[]{:S(2)}) async-start(bf16[32,2,1152]{2,1,0:T(2,128)(2,1)} %reshape.319), calls=%async_computation.1 | async-start | bytes 294912 | tf_op jit(solution)/shard_map/while/body/eval_jaxpr/all_to_all | solution.py:140
  437.0 14.5 %all-to-all-start.2 = ((bf16[32,2,1152]{2,1,0:T(2,128)(2,1)}), bf16[32,2,1152]{2,1,0:T(2,128)(2,1)S(1)}, u32[]{:S(2)}, u32[]{:S(2)}) async-start(bf16[32,2,1152]{2,1,0:T(2,128)(2,1)} %reshape.323), calls=%async_computation.2 | async-start | bytes 294912 | tf_op jit(solution)/shard_map/while/body/eval_jaxpr/all_to_all | solution.py:141
  506.4 18.3 %all-to-all-start.1 = ((bf16[32,2,1152]{2,1,0:T(2,128)(2,1)}), bf16[32,2,1152]{2,1,0:T(2,128)(2,1)S(1)}, u32[]{:S(2)}, u32[]{:S(2)}) async-start(bf16[32,2,1152]{2,1,0:T(2,128)(2,1)} %reshape.319), calls=%async_computation.1 | async-start | bytes 294912 | tf_op jit(solution)/shard_map/while/body/eval_jaxpr/all_to_all | solution.py:140
  524.7 14.5 %all-to-all-start.2 = ((bf16[32,2,1152]{2,1,0:T(2,128)(2,1)}), bf16[32,2,1152]{2,1,0:T(2,128)(2,1)S(1)}, u32[]{:S(2)}, u32[]{:S(2)}) async-start(bf16[32,2,1152]{2,1,0:T(2,128)(2,1)} %reshape.323), calls=%async_computation.2 | async-start | bytes 294912 | tf_op jit(solution)/shard_map/while/body/eval_jaxpr/all_to_all | solution.py:141
  594.6 18.3 %all-to-all-start.1 = ((bf16[32,2,1152]{2,1,0:T(2,128)(2,1)}), bf16[32,2,1152]{2,1,0:T(2,128)(2,1)S(1)}, u32[]{:S(2)}, u32[]{:S(2)}) async-start(bf16[32,2,1152]{2,1,0:T(2,128)(2,1)} %reshape.319), calls=%async_computation.1 | async-start | bytes 294912 | tf_op jit(solution)/shard_map/while/body/eval_jaxpr/all_to_all | solution.py:140
  682.4 18.3 %all-to-all-start.1 = ((bf16[32,2,1152]{2,1,0:T(2,128)(2,1)}), bf16[32,2,1152]{2,1,0:T(2,128)(2,1)S(1)}, u32[]{:S(2)}, u32[]{:S(2)}) async-start(bf16[32,2,1152]{2,1,0:T(2,128)(2,1)} %reshape.319), calls=%async_computation.1 | async-start | bytes 294912 | tf_op jit(solution)/shard_map/while/body/eval_jaxpr/all_to_all | solution.py:140
  700.7 14.5 %all-to-all-start.2 = ((bf16[32,2,1152]{2,1,0:T(2,128)(2,1)}), bf16[32,2,1152]{2,1,0:T(2,128)(2,1)S(1)}, u32[]{:S(2)}, u32[]{:S(2)}) async-start(bf16[32,2,1152]{2,1,0:T(2,128)(2,1)} %reshape.323), calls=%async_computation.2 | async-start | bytes 294912 | tf_op jit(solution)/shard_map/while/body/eval_jaxpr/all_to_all | solution.py:141
  770.7 18.3 %all-to-all-start.1 = ((bf16[32,2,1152]{2,1,0:T(2,128)(2,1)}), bf16[32,2,1152]{2,1,0:T(2,128)(2,1)S(1)}, u32[]{:S(2)}, u32[]{:S(2)}) async-start(bf16[32,2,1152]{2,1,0:T(2,128)(2,1)} %reshape.319), calls=%async_computation.1 | async-start | bytes 294912 | tf_op jit(solution)/shard_map/while/body/eval_jaxpr/all_to_all | solution.py:140
  858.4 18.3 %all-to-all-start.1 = ((bf16[32,2,1152]{2,1,0:T(2,128)(2,1)}), bf16[32,2,1152]{2,1,0:T(2,128)(2,1)S(1)}, u32[]{:S(2)}, u32[]{:S(2)}) async-start(bf16[32,2,1152]{2,1,0:T(2,128)(2,1)} %reshape.319), calls=%async_computation.1 | async-start | bytes 294912 | tf_op jit(solution)/shard_map/while/body/eval_jaxpr/all_to_all | solution.py:140
  876.8 14.5 %all-to-all-start.2 = ((bf16[32,2,1152]{2,1,0:T(2,128)(2,1)}), bf16[32,2,1152]{2,1,0:T(2,128)(2,1)S(1)}, u32[]{:S(2)}, u32[]{:S(2)}) async-start(bf16[32,2,1152]{2,1,0:T(2,128)(2,1)} %reshape.323), calls=%async_computation.2 | async-start | bytes 294912 | tf_op jit(solution)/shard_map/while/body/eval_jaxpr/all_to_all | solution.py:141
  946.7 18.7 %all-to-all-start.1 = ((bf16[32,2,1152]{2,1,0:T(2,128)(2,1)}), bf16[32,2,1152]{2,1,0:T(2,128)(2,1)S(1)}, u32[]{:S(2)}, u32[]{:S(2)}) async-start(bf16[32,2,1152]{2,1,0:T(2,128)(2,1)} %reshape.319), calls=%async_computation.1 | async-start | bytes 294912 | tf_op jit(solution)/shard_map/while/body/eval_jaxpr/all_to_all | solution.py:140
  965.4 14.7 %all-to-all-start.2 = ((bf16[32,2,1152]{2,1,0:T(2,128)(2,1)}), bf16[32,2,1152]{2,1,0:T(2,128)(2,1)S(1)}, u32[]{:S(2)}, u32[]{:S(2)}) async-start(bf16[32,2,1152]{2,1,0:T(2,128)(2,1)} %reshape.323), calls=%async_computation.2 | async-start | bytes 294912 | tf_op jit(solution)/shard_map/while/body/eval_jaxpr/all_to_all | solution.py:141
  1035.0 18.3 %all-to-all-start.1 = ((bf16[32,2,1152]{2,1,0:T(2,128)(2,1)}), bf16[32,2,1152]{2,1,0:T(2,128)(2,1)S(1)}, u32[]{:S(2)}, u32[]{:S(2)}) async-start(bf16[32,2,1152]{2,1,0:T(2,128)(2,1)} %reshape.319), calls=%async_computation.1 | async-start | bytes 294912 | tf_op jit(solution)/shard_map/while/body/eval_jaxpr/all_to_all | solution.py:140
  1053.3 14.5 %all-to-all-start.2 = ((bf16[32,2,1152]{2,1,0:T(2,128)(2,1)}), bf16[32,2,1152]{2,1,0:T(2,128)(2,1)S(1)}, u32[]{:S(2)}, u32[]{:S(2)}) async-start(bf16[32,2,1152]{2,1,0:T(2,128)(2,1)} %reshape.323), calls=%async_computation.2 | async-start | bytes 294912 | tf_op jit(solution)/shard_map/while/body/eval_jaxpr/all_to_all | solution.py:141
  1123.2 18.3 %all-to-all-start.1 = ((bf16[32,2,1152]{2,1,0:T(2,128)(2,1)}), bf16[32,2,1152]{2,1,0:T(2,128)(2,1)S(1)}, u32[]{:S(2)}, u32[]{:S(2)}) async-start(bf16[32,2,1152]{2,1,0:T(2,128)(2,1)} %reshape.319), calls=%async_computation.1 | async-start | bytes 294912 | tf_op jit(solution)/shard_map/while/body/eval_jaxpr/all_to_all | solution.py:140
  1210.9 18.3 %all-to-all-start.1 = ((bf16[32,2,1152]{2,1,0:T(2,128)(2,1)}), bf16[32,2,1152]{2,1,0:T(2,128)(2,1)S(1)}, u32[]{:S(2)}, u32[]{:S(2)}) async-start(bf16[32,2,1152]{2,1,0:T(2,128)(2,1)} %reshape.319), calls=%async_computation.1 | async-start | bytes 294912 | tf_op jit(solution)/shard_map/while/body/eval_jaxpr/all_to_all | solution.py:140
  1229.3 14.5 %all-to-all-start.2 = ((bf16[32,2,1152]{2,1,0:T(2,128)(2,1)}), bf16[32,2,1152]{2,1,0:T(2,128)(2,1)S(1)}, u32[]{:S(2)}, u32[]{:S(2)}) async-start(bf16[32,2,1152]{2,1,0:T(2,128)(2,1)} %reshape.323), calls=%async_computation.2 | async-start | bytes 294912 | tf_op jit(solution)/shard_map/while/body/eval_jaxpr/all_to_all | solution.py:141
  (60 other events, 735.0 us)
Sparse Core Ops, SparseCore 0:
  9.2 34.6 all-gather.5
  45.7 17.5 all-gather.3
  65.1 21.0 all-gather.7
where the time goes:
time: 1280 us
  starting transfers between devices  331 us (26%)
  waiting for transfers between devices  301 us (24%)
  matrix products  225 us (18%)
  blocking collectives  181 us (14%)
  local copies, waits for them, and re-layouts  112 us (9%)
  other arithmetic  97.6 us (8%)
  loops' own time  18.3 us (1%)
  between operations  13.9 us (1%)
    unnamed x1, blocking collectives  181 us
    all_to_all x12, starting transfers between devices, one_turn(): lax.all_to_all(key_units(joined_keys), 'seq', split_axis=0, concat_axis=1...  113 us
    all_to_all x12, waiting for transfers between devices, one_turn(): lax.all_to_all(attended.reshape(unit_here, seq_count * query_rows * head_...  97.6 us
    all_to_all x12, waiting for transfers between devices, one_turn(): lax.all_to_all(key_units(joined_values), 'seq', split_axis=0, concat_axis...  86.2 us
    dot_general x12, matrix products, one_turn(): jnp.dot(normed, attn_weight, preferred_element_type=jnp.float32)  84.3 us
    all_to_all x12, waiting for transfers between devices, one_turn(): lax.all_to_all(key_units(joined_keys), 'seq', split_axis=0, concat_axis=1...  68.3 us
    all_to_all x12, starting transfers between devices, one_turn(): lax.all_to_all(attended.reshape(unit_here, seq_count * query_rows * head_...  66.6 us
    all_to_all x12, starting transfers between devices, one_turn(): lax.all_to_all(key_units(joined_values), 'seq', split_axis=0, concat_axis...  65.9 us
  transfers between devices with their start and end apart: 75, of which 60 were waited for; matrix products, arithmetic and copies ran while one was open for 14% of the time, Pallas kernels for 0%

commit v1 on v0

--- a/solution.py
+++ b/solution.py
@@ -158,12 +158,20 @@
         attended = jnp.einsum(
             "uqk,ukc->uqc", weights, all_values, preferred_element_type=jnp.float32
         ).astype(jnp.bfloat16)
-        returned = lax.all_to_all(
-            attended.reshape(unit_here, seq_count * query_rows * head_size),
-            "seq",
-            split_axis=1,
-            concat_axis=0,
-            tiled=True,
+        returned = jnp.concatenate(
+            lax.all_to_all(
+                jnp.stack(
+                    jnp.split(
+                        attended.reshape(unit_here, seq_count * query_rows * head_size),
+                        lax.axis_size("seq"),
+                        axis=1,
+                    )
+                ),
+                "seq",
+                0,
+                0,
+            ),
+            axis=0,
         )
         merged_heads = from_units(returned)
         update = jnp.dot(merged_heads, proj_weight, preferred_element_type=jnp.float32)

time: 1280 us -> 1290 us (level)
    while x108 -> x468, local copies, waits for them, and re-layouts: 41.6 us -> 39.4 us
where the time goes in v1:
time: 1290 us
  starting transfers between devices  331 us (26%)
  waiting for transfers between devices  301 us (23%)
  matrix products  225 us (17%)
  blocking collectives  181 us (14%)
  local copies, waits for them, and re-layouts  114 us (9%)
  other arithmetic  101 us (8%)
  loops' own time  19.6 us (2%)
  between operations  13.9 us (1%)
    unnamed x1, blocking collectives  181 us
    all_to_all x12, starting transfers between devices, one_turn(): lax.all_to_all(key_units(joined_keys), 'seq', split_axis=0, concat_axis=1...  113 us
    all_to_all x12, waiting for transfers between devices, one_turn(): lax.all_to_all(jnp.stack(jnp.split(attended.reshape(unit_here, seq_count...  97.7 us
    all_to_all x12, waiting for transfers between devices, one_turn(): lax.all_to_all(key_units(joined_values), 'seq', split_axis=0, concat_axis...  86.2 us
    dot_general x12, matrix products, one_turn(): jnp.dot(normed, attn_weight, preferred_element_type=jnp.float32)  84.3 us
    all_to_all x12, waiting for transfers between devices, one_turn(): lax.all_to_all(key_units(joined_keys), 'seq', split_axis=0, concat_axis=1...  68.2 us
    all_to_all x12, starting transfers between devices, one_turn(): lax.all_to_all(jnp.stack(jnp.split(attended.reshape(unit_here, seq_count...  66.5 us
    all_to_all x12, starting transfers between devices, one_turn(): lax.all_to_all(key_units(joined_values), 'seq', split_axis=0, concat_axis...  65.9 us
  transfers between devices with their start and end apart: 75, of which 60 were waited for; matrix products, arithmetic and copies ran while one was open for 14% of the time, Pallas kernels for 0%

profile of v1, /device:TPU:8, one launch (start us, length us, event | category | flops | bytes accessed | tf_op | source)
XLA Modules:
  0.0 1286.0 jit_solution(8186045856491485714)
XLA Ops:
  21.8 181.4 %all-reduce.3 = bf16[256,4,1536]{2,1,0:T(4,128)(2,1)} all-reduce(f32[256,4,1536]{2,1,0:T(4,128)} %copy.40), channel_id=2, replica_groups=mesh['pipe'=4,'seq'=32,'batch'=2] {'seq'}, use_global_device_ids=true, to_apply=%region_0.0.clone | all-reduce | flops 1572864 | bytes 9437184
  204.3 8.1 slice.137
  212.5 1066.4 %while.17 = (s32[]{:T(128)}, bf16[16,1536]{1,0:T(8,128)(2,1)S(1)}, f32[16,64]{1,0:T(8,128)S(1)}, s32[]{:T(128)}, pred[]{:T(512)}, /*index=5*/bf16[64,1536]{1,0:T...) while((s32[]{:T(128)}, bf16[16,1536]{1,0:T(8,128)(2,1)S(1)}, ...), condition=%wide.region_10.11_spmd, body=%wide.region_1.10_spmd.sunk | while | flops 464863840 | bytes 44026800 | solution.py:193
  225.9 9.6 all-to-all-start
  244.2 9.4 all-to-all-start.1
  288.1 8.1 all-to-all-done.3
  332.3 9.4 all-to-all-start.1
  376.3 8.1 all-to-all-done.3
  421.0 9.4 all-to-all-start.1
  464.9 8.1 all-to-all-done.3
  509.1 9.4 all-to-all-start.1
  597.7 9.4 all-to-all-start.1
  641.7 8.1 all-to-all-done.3
  685.9 9.4 all-to-all-start.1
  729.9 8.2 all-to-all-done.3
  774.8 9.4 all-to-all-start.1
  863.0 9.4 all-to-all-start.1
  907.0 8.1 all-to-all-done.3
  951.5 9.4 all-to-all-start.1
  996.1 8.1 all-to-all-done.3
  1040.3 9.4 all-to-all-start.1
  1129.0 9.4 all-to-all-start.1
  1217.2 9.4 all-to-all-start.1
  1261.2 8.1 all-to-all-done.3
  (1393 shorter events, 875.2 us)
Async XLA Ops:
  6.5 197.7 %all-gather.6.cloned.1.call-start = ((), (), s32[]{:S(2)}) async-start(), calls=%async_computation.5 | async-start | bytes 21233664 | tf_op jit(solution)/shard_map/all_gather | solution.py:53
  7.3 205.2 %all-gather.4.cloned.1.call-start = ((), (), s32[]{:S(2)}) async-start(), calls=%async_computation.4 | async-start | bytes 3538944 | tf_op jit(solution)/shard_map/all_gather | solution.py:55
  8.0 204.4 %all-gather.8.cloned.1.call-start = ((), (), s32[]{:S(2)}) async-start(), calls=%async_computation.6 | async-start | bytes 7077888 | tf_op jit(solution)/shard_map/all_gather | solution.py:54
  225.9 18.3 %all-to-all-start = ((bf16[32,2,384]{2,1,0:T(2,128)(2,1)}), bf16[32,2,384]{2,1,0:T(2,128)(2,1)S(1)}, u32[]{:S(2)}, u32[]{:S(2)}) async-start(bf16[32,2,384]{2,1,0:T(2,128)(2,1)} %reshape.310), calls=%async_computation | async-start | bytes 98304 | tf_op jit(solution)/shard_map/while/body/eval_jaxpr/all_to_all | solution.py:139
  244.2 18.3 %all-to-all-start.1 = ((bf16[32,2,1152]{2,1,0:T(2,128)(2,1)}), bf16[32,2,1152]{2,1,0:T(2,128)(2,1)S(1)}, u32[]{:S(2)}, u32[]{:S(2)}) async-start(bf16[32,2,1152]{2,1,0:T(2,128)(2,1)} %reshape.314), calls=%async_computation.1 | async-start | bytes 294912 | tf_op jit(solution)/shard_map/while/body/eval_jaxpr/all_to_all | solution.py:140
  262.5 14.5 %all-to-all-start.2 = ((bf16[32,2,1152]{2,1,0:T(2,128)(2,1)}), bf16[32,2,1152]{2,1,0:T(2,128)(2,1)S(1)}, u32[]{:S(2)}, u32[]{:S(2)}) async-start(bf16[32,2,1152]{2,1,0:T(2,128)(2,1)} %reshape.318), calls=%async_computation.2 | async-start | bytes 294912 | tf_op jit(solution)/shard_map/while/body/eval_jaxpr/all_to_all | solution.py:141
  332.3 18.3 %all-to-all-start.1 = ((bf16[32,2,1152]{2,1,0:T(2,128)(2,1)}), bf16[32,2,1152]{2,1,0:T(2,128)(2,1)S(1)}, u32[]{:S(2)}, u32[]{:S(2)}) async-start(bf16[32,2,1152]{2,1,0:T(2,128)(2,1)} %reshape.314), calls=%async_computation.1 | async-start | bytes 294912 | tf_op jit(solution)/shard_map/while/body/eval_jaxpr/all_to_all | solution.py:140
  350.7 14.5 %all-to-all-start.2 = ((bf16[32,2,1152]{2,1,0:T(2,128)(2,1)}), bf16[32,2,1152]{2,1,0:T(2,128)(2,1)S(1)}, u32[]{:S(2)}, u32[]{:S(2)}) async-start(bf16[32,2,1152]{2,1,0:T(2,128)(2,1)} %reshape.318), calls=%async_computation.2 | async-start | bytes 294912 | tf_op jit(solution)/shard_map/while/body/eval_jaxpr/all_to_all | solution.py:141
  421.0 18.3 %all-to-all-start.1 = ((bf16[32,2,1152]{2,1,0:T(2,128)(2,1)}), bf16[32,2,1152]{2,1,0:T(2,128)(2,1)S(1)}, u32[]{:S(2)}, u32[]{:S(2)}) async-start(bf16[32,2,1152]{2,1,0:T(2,128)(2,1)} %reshape.314), calls=%async_computation.1 | async-start | bytes 294912 | tf_op jit(solution)/shard_map/while/body/eval_jaxpr/all_to_all | solution.py:140
  509.1 18.3 %all-to-all-start.1 = ((bf16[32,2,1152]{2,1,0:T(2,128)(2,1)}), bf16[32,2,1152]{2,1,0:T(2,128)(2,1)S(1)}, u32[]{:S(2)}, u32[]{:S(2)}) async-start(bf16[32,2,1152]{2,1,0:T(2,128)(2,1)} %reshape.314), calls=%async_computation.1 | async-start | bytes 294912 | tf_op jit(solution)/shard_map/while/body/eval_jaxpr/all_to_all | solution.py:140
  527.4 14.5 %all-to-all-start.2 = ((bf16[32,2,1152]{2,1,0:T(2,128)(2,1)}), bf16[32,2,1152]{2,1,0:T(2,128)(2,1)S(1)}, u32[]{:S(2)}, u32[]{:S(2)}) async-start(bf16[32,2,1152]{2,1,0:T(2,128)(2,1)} %reshape.318), calls=%async_computation.2 | async-start | bytes 294912 | tf_op jit(solution)/shard_map/while/body/eval_jaxpr/all_to_all | solution.py:141
  597.7 18.3 %all-to-all-start.1 = ((bf16[32,2,1152]{2,1,0:T(2,128)(2,1)}), bf16[32,2,1152]{2,1,0:T(2,128)(2,1)S(1)}, u32[]{:S(2)}, u32[]{:S(2)}) async-start(bf16[32,2,1152]{2,1,0:T(2,128)(2,1)} %reshape.314), calls=%async_computation.1 | async-start | bytes 294912 | tf_op jit(solution)/shard_map/while/body/eval_jaxpr/all_to_all | solution.py:140
  685.9 18.3 %all-to-all-start.1 = ((bf16[32,2,1152]{2,1,0:T(2,128)(2,1)}), bf16[32,2,1152]{2,1,0:T(2,128)(2,1)S(1)}, u32[]{:S(2)}, u32[]{:S(2)}) async-start(bf16[32,2,1152]{2,1,0:T(2,128)(2,1)} %reshape.314), calls=%async_computation.1 | async-start | bytes 294912 | tf_op jit(solution)/shard_map/while/body/eval_jaxpr/all_to_all | solution.py:140
  704.3 14.5 %all-to-all-start.2 = ((bf16[32,2,1152]{2,1,0:T(2,128)(2,1)}), bf16[32,2,1152]{2,1,0:T(2,128)(2,1)S(1)}, u32[]{:S(2)}, u32[]{:S(2)}) async-start(bf16[32,2,1152]{2,1,0:T(2,128)(2,1)} %reshape.318), calls=%async_computation.2 | async-start | bytes 294912 | tf_op jit(solution)/shard_map/while/body/eval_jaxpr/all_to_all | solution.py:141
  774.8 18.3 %all-to-all-start.1 = ((bf16[32,2,1152]{2,1,0:T(2,128)(2,1)}), bf16[32,2,1152]{2,1,0:T(2,128)(2,1)S(1)}, u32[]{:S(2)}, u32[]{:S(2)}) async-start(bf16[32,2,1152]{2,1,0:T(2,128)(2,1)} %reshape.314), calls=%async_computation.1 | async-start | bytes 294912 | tf_op jit(solution)/shard_map/while/body/eval_jaxpr/all_to_all | solution.py:140
  863.0 18.3 %all-to-all-start.1 = ((bf16[32,2,1152]{2,1,0:T(2,128)(2,1)}), bf16[32,2,1152]{2,1,0:T(2,128)(2,1)S(1)}, u32[]{:S(2)}, u32[]{:S(2)}) async-start(bf16[32,2,1152]{2,1,0:T(2,128)(2,1)} %reshape.314), calls=%async_computation.1 | async-start | bytes 294912 | tf_op jit(solution)/shard_map/while/body/eval_jaxpr/all_to_all | solution.py:140
  951.5 18.5 %all-to-all-start.1 = ((bf16[32,2,1152]{2,1,0:T(2,128)(2,1)}), bf16[32,2,1152]{2,1,0:T(2,128)(2,1)S(1)}, u32[]{:S(2)}, u32[]{:S(2)}) async-start(bf16[32,2,1152]{2,1,0:T(2,128)(2,1)} %reshape.314), calls=%async_computation.1 | async-start | bytes 294912 | tf_op jit(solution)/shard_map/while/body/eval_jaxpr/all_to_all | solution.py:140
  970.1 14.8 %all-to-all-start.2 = ((bf16[32,2,1152]{2,1,0:T(2,128)(2,1)}), bf16[32,2,1152]{2,1,0:T(2,128)(2,1)S(1)}, u32[]{:S(2)}, u32[]{:S(2)}) async-start(bf16[32,2,1152]{2,1,0:T(2,128)(2,1)} %reshape.318), calls=%async_computation.2 | async-start | bytes 294912 | tf_op jit(solution)/shard_map/while/body/eval_jaxpr/all_to_all | solution.py:141
  1040.3 18.3 %all-to-all-start.1 = ((bf16[32,2,1152]{2,1,0:T(2,128)(2,1)}), bf16[32,2,1152]{2,1,0:T(2,128)(2,1)S(1)}, u32[]{:S(2)}, u32[]{:S(2)}) async-start(bf16[32,2,1152]{2,1,0:T(2,128)(2,1)} %reshape.314), calls=%async_computation.1 | async-start | bytes 294912 | tf_op jit(solution)/shard_map/while/body/eval_jaxpr/all_to_all | solution.py:140
  1058.7 14.5 %all-to-all-start.2 = ((bf16[32,2,1152]{2,1,0:T(2,128)(2,1)}), bf16[32,2,1152]{2,1,0:T(2,128)(2,1)S(1)}, u32[]{:S(2)}, u32[]{:S(2)}) async-start(bf16[32,2,1152]{2,1,0:T(2,128)(2,1)} %reshape.318), calls=%async_computation.2 | async-start | bytes 294912 | tf_op jit(solution)/shard_map/while/body/eval_jaxpr/all_to_all | solution.py:141
  1129.0 18.3 %all-to-all-start.1 = ((bf16[32,2,1152]{2,1,0:T(2,128)(2,1)}), bf16[32,2,1152]{2,1,0:T(2,128)(2,1)S(1)}, u32[]{:S(2)}, u32[]{:S(2)}) async-start(bf16[32,2,1152]{2,1,0:T(2,128)(2,1)} %reshape.314), calls=%async_computation.1 | async-start | bytes 294912 | tf_op jit(solution)/shard_map/while/body/eval_jaxpr/all_to_all | solution.py:140
  1147.3 14.5 %all-to-all-start.2 = ((bf16[32,2,1152]{2,1,0:T(2,128)(2,1)}), bf16[32,2,1152]{2,1,0:T(2,128)(2,1)S(1)}, u32[]{:S(2)}, u32[]{:S(2)}) async-start(bf16[32,2,1152]{2,1,0:T(2,128)(2,1)} %reshape.318), calls=%async_computation.2 | async-start | bytes 294912 | tf_op jit(solution)/shard_map/while/body/eval_jaxpr/all_to_all | solution.py:141
  1217.2 18.3 %all-to-all-start.1 = ((bf16[32,2,1152]{2,1,0:T(2,128)(2,1)}), bf16[32,2,1152]{2,1,0:T(2,128)(2,1)S(1)}, u32[]{:S(2)}, u32[]{:S(2)}) async-start(bf16[32,2,1152]{2,1,0:T(2,128)(2,1)} %reshape.314), calls=%async_computation.1 | async-start | bytes 294912 | tf_op jit(solution)/shard_map/while/body/eval_jaxpr/all_to_all | solution.py:140
  1235.6 14.5 %all-to-all-start.2 = ((bf16[32,2,1152]{2,1,0:T(2,128)(2,1)}), bf16[32,2,1152]{2,1,0:T(2,128)(2,1)S(1)}, u32[]{:S(2)}, u32[]{:S(2)}) async-start(bf16[32,2,1152]{2,1,0:T(2,128)(2,1)} %reshape.318), calls=%async_computation.2 | async-start | bytes 294912 | tf_op jit(solution)/shard_map/while/body/eval_jaxpr/all_to_all | solution.py:141
  (60 other events, 736.2 us)
Sparse Core Ops, SparseCore 0:
  9.2 34.6 all-gather.5
  45.7 17.5 all-gather.3
  65.1 21.0 all-gather.7
